TPU v7x, 32 devices: a whole 2x2x4 slice. The times are simulated.
32 devices in a mesh: ctx: 8 (over z, x), dp: 4 (over y, core).
Axes of the slice: x: 2, y: 2, z: 4, core: 2. Of those that a mesh axis runs over, the one named last changes fastest.
Arguments:
- queries: bfloat16 [4, 1024, 2048], P('dp', 'ctx'), may hold values from -400 to 400
- keys: bfloat16 [4, 1024, 1024], P('dp', 'ctx'), may hold values from -400 to 400
- values: bfloat16 [4, 1024, 1024], P('dp', 'ctx'), may hold values from -6 to 6
- q_gain: float32 [256], replicated, may hold values from 0.25 to 1.75
- key_norm_gain: float32 [256], replicated, may hold values from 0.25 to 1.75
- segment_ids: int32 [4, 1024], P('dp', 'ctx'), may hold values from 0 to 3, never falling along the last dimension, each value on 1 to 512 neighbouring positions
- output_gradient: bfloat16 [4, 1024, 2048], P('dp', 'ctx'), may hold values from -14 to 14
Outputs:
- attn_out: bfloat16 [4, 1024, 2048], P('dp', 'ctx')
- grad_queries: bfloat16 [4, 1024, 2048], P('dp', 'ctx')
- key_gradient: bfloat16 [4, 1024, 1024], P('dp', 'ctx')
- value_gradient: bfloat16 [4, 1024, 1024], P('dp', 'ctx')
- grad_q_gain: float32 [256], replicated
- grad_k_gain: float32 [256], replicated
Inputs may be any that keep to these rules, and one draw needn't show every extreme that they name: `segment_ids`: document ids never fall along a sequence; every id from 0 to 3 is used, each document holds 1 to 512 tokens and at least one holds exactly 512.
All inputs are finite; a program needn't handle non-finite values.
Results may differ from a plain program's by a relative error of at most 0.013.
Values may be sent and summed in bfloat16 or wider, within the bound.
A program may use at most 64 MiB of HBM per device.

v0:
```python
import jax
import jax.numpy as jnp
from jax import lax
from jax.sharding import PartitionSpec as P

QUERY_HEADS = 8
KEY_VALUE_HEADS = 4
HEAD_SIZE = 256
WINDOW = 256
HALO = 2


EPS = 1e-06


def shifted(value, axis, by):
    count = lax.axis_size(axis)
    pairs = [(i, i + by) for i in range(count) if 0 <= i + by < count]
    return lax.ppermute(value, axis, pairs)


def rms_normalize(inputs, heads, gain_vec):
    as_float = inputs.astype(jnp.float32).reshape(inputs.shape[0], heads, HEAD_SIZE)
    inv_rms = lax.rsqrt(jnp.mean(as_float * as_float, -1, keepdims=True) + EPS)
    normed = as_float * inv_rms
    return (normed, inv_rms, (normed * gain_vec).astype(jnp.bfloat16))


def rms_norm_backward(upstream, normed, inv_rms, gain_vec):
    scaled = upstream * gain_vec
    return inv_rms * (scaled - normed * jnp.mean(scaled * normed, -1, keepdims=True))


def body(queries, keys, values, q_gain, key_norm_gain, segment_ids, output_gradient):
    token_rows = queries.shape[1]
    query_group_width = QUERY_HEADS // KEY_VALUE_HEADS
    score_scale = HEAD_SIZE ** (-0.5)
    ctx_index = lax.axis_index("ctx")
    q_normed, q_inv, query_norm_result = rms_normalize(queries[0], QUERY_HEADS, q_gain)
    normalized_keys, key_inverse_rms, key_norm_result = rms_normalize(
        keys[0], KEY_VALUE_HEADS, key_norm_gain
    )
    own_seg = segment_ids[0]
    local_key_value = jnp.stack(
        [key_norm_result.reshape(token_rows, KEY_VALUE_HEADS * HEAD_SIZE), values[0]]
    )
    received = []
    for offset in range(1, HALO + 1):
        received.append(shifted((local_key_value, own_seg), "ctx", offset))
    blocks = [received[HALO - 1 - block] for block in range(HALO)] + [(local_key_value, own_seg)]
    positions = jnp.arange(token_rows, dtype=jnp.int32)
    q_pos = ctx_index * token_rows + positions
    grouped_queries = query_norm_result.reshape(
        token_rows, KEY_VALUE_HEADS, query_group_width, HEAD_SIZE
    )
    key_block_list, value_block_list, key_masks, live_flags = ([], [], [], [])
    for block in range(HALO + 1):
        key_value_pair, seg_block = blocks[block]
        k_pos = (ctx_index - HALO + block) * token_rows + positions
        distance = q_pos[:, None] - k_pos[None, :]
        key_mask = (
            (distance >= 0)
            & (distance < WINDOW)
            & (k_pos[None, :] >= 0)
            & (own_seg[:, None] == seg_block[None, :])
        )
        key_block_list.append(key_value_pair[0].reshape(token_rows, KEY_VALUE_HEADS, HEAD_SIZE))
        value_block_list.append(key_value_pair[1].reshape(token_rows, KEY_VALUE_HEADS, HEAD_SIZE))
        key_masks.append(key_mask)
        live_flags.append(jnp.any(key_mask))
    output_shape = (token_rows, KEY_VALUE_HEADS, query_group_width, HEAD_SIZE)

    def exp_block(block):
        scores = (
            jnp.einsum(
                "qhgd,khd->hgqk",
                grouped_queries,
                key_block_list[block],
                preferred_element_type=jnp.float32,
            )
            * score_scale
        )
        return jnp.where(key_masks[block], jnp.exp(scores), 0.0)

    exp_blocks = [exp_block(block) for block in range(HALO + 1)]
    row_totals = sum((jnp.sum(exp_value, -1) for exp_value in exp_blocks))[..., None]
    prob_b_blocks = [(exp_value / row_totals).astype(jnp.bfloat16) for exp_value in exp_blocks]

    def attend_block(block):
        return jnp.einsum(
            "hgqk,khd->qhgd",
            prob_b_blocks[block],
            value_block_list[block],
            preferred_element_type=jnp.float32,
        )

    attn_sum = sum((attend_block(block) for block in range(HALO + 1)))
    attn_out = attn_sum.astype(jnp.bfloat16)
    grad_out = output_gradient[0].reshape(output_shape)
    row_delta = jnp.sum(grad_out.astype(jnp.float32) * attn_out.astype(jnp.float32), -1).transpose(
        1, 2, 0
    )

    def backward_block(block):
        prob_grad = jnp.einsum(
            "qhgd,khd->hgqk", grad_out, value_block_list[block], preferred_element_type=jnp.float32
        )
        score_grad = (exp_blocks[block] / row_totals * (prob_grad - row_delta[..., None])).astype(
            jnp.bfloat16
        )
        q_part = jnp.einsum(
            "hgqk,khd->qhgd", score_grad, key_block_list[block], preferred_element_type=jnp.float32
        )
        key_term = (
            jnp.einsum(
                "hgqk,qhgd->khd", score_grad, grouped_queries, preferred_element_type=jnp.float32
            )
            * score_scale
        ).astype(jnp.bfloat16)
        value_term = jnp.einsum(
            "hgqk,qhgd->khd", prob_b_blocks[block], grad_out, preferred_element_type=jnp.float32
        ).astype(jnp.bfloat16)
        return (q_part, key_term, value_term)

    back_blocks = [backward_block(block) for block in range(HALO + 1)]
    q_grad_norm = (sum((item[0] for item in back_blocks)) * score_scale).reshape(
        token_rows, QUERY_HEADS, HEAD_SIZE
    )
    key_acc = back_blocks[HALO][1].astype(jnp.float32)
    value_accumulator = back_blocks[HALO][2].astype(jnp.float32)
    for offset in range(1, HALO + 1):
        block = HALO - offset
        returned = shifted(
            jnp.stack([back_blocks[block][1], back_blocks[block][2]]), "ctx", -offset
        )
        key_acc = key_acc + returned[0].astype(jnp.float32)
        value_accumulator = value_accumulator + returned[1].astype(jnp.float32)
    grad_queries = (
        rms_norm_backward(q_grad_norm, q_normed, q_inv, q_gain)
        .astype(jnp.bfloat16)
        .reshape(1, token_rows, QUERY_HEADS * HEAD_SIZE)
    )
    key_gradient = (
        rms_norm_backward(key_acc, normalized_keys, key_inverse_rms, key_norm_gain)
        .astype(jnp.bfloat16)
        .reshape(1, token_rows, KEY_VALUE_HEADS * HEAD_SIZE)
    )
    value_gradient = value_accumulator.astype(jnp.bfloat16).reshape(
        1, token_rows, KEY_VALUE_HEADS * HEAD_SIZE
    )
    q_sum_part = jnp.sum(q_grad_norm * q_normed, (0, 1))
    k_sum_part = jnp.sum(key_acc * normalized_keys, (0, 1))
    q_total, k_total = lax.psum((q_sum_part, k_sum_part), ("ctx", "dp"))
    factor = (lax.axis_size("ctx") * lax.axis_size("dp") * token_rows) ** (-0.5)
    return (
        attn_out.reshape(1, token_rows, QUERY_HEADS * HEAD_SIZE),
        grad_queries,
        key_gradient,
        value_gradient,
        q_total * factor,
        k_total * factor,
    )


def solution(mesh):
    placed = (
        P("dp", "ctx", None),
        P("dp", "ctx", None),
        P("dp", "ctx", None),
        P(),
        P(),
        P("dp", "ctx"),
        P("dp", "ctx", None),
    )
    return jax.shard_map(
        body,
        mesh=mesh,
        in_specs=placed,
        out_specs=(
            P("dp", "ctx", None),
            P("dp", "ctx", None),
            P("dp", "ctx", None),
            P("dp", "ctx", None),
            P(),
            P(),
        ),
        check_vma=False,
    )
```

profile of v0, /device:TPU:0, one launch (start us, length us, event | category | flops | bytes accessed | tf_op | source)
XLA Modules:
  0.0 116.2 jit_solution(12190796642584265772)
XLA Ops:
  1.3 4.9 %collective-permute-start.1 = (s32[128]{0:T(128)S(1)}, s32[128]{0:T(128)S(1)}, u32[]{:S(2)}, u32[]{:S(2)}) collective-permute-start(s32[128]{0:T(128)S(1)} %bitcast.294), channel_id=1, source_target_pairs={{0,8},{4,12},{8,16},{12,20},{16,24},{20,28},{1,9},{5,13},{9,17},{1... | collective-permute-start | bytes 1544 | tf_op jit(solution)/shard_map/ppermute | solution.py:19
  6.2 3.4 %collective-permute-start.2 = (s32[128]{0:T(128)S(1)}, s32[128]{0:T(128)S(1)}, u32[]{:S(2)}, u32[]{:S(2)}) collective-permute-start(s32[128]{0:T(128)S(1)} %bitcast.295), channel_id=1, source_target_pairs={{0,4},{4,8},{8,12},{12,16},{16,20},{20,24},{24,28},{1,5},{5,9},{9,... | collective-permute-start | bytes 1544 | tf_op jit(solution)/shard_map/ppermute | solution.py:19
  9.6 1.1 copy.170
  12.1 0.8 pad_maximum_fusion
  12.9 4.3 %collective-permute-start = (bf16[2,128,1024]{1,2,0:T(8,128)(2,1)}, bf16[2,128,1024]{1,2,0:T(8,128)(2,1)}, u32[]{:S(2)}, u32[]{:S(2)}) collective-permute-start(bf16[2,128,1024]{1,2,0:T(8,128)(2,1)} %pad_maximum_fusion), channel_id=1, source_target_pairs={{0,8},{4,12},{8,16},{12,20},{16,24},{20,28},{1,9},{5,13},{9,17},{1... | collective-permute-start | bytes 1572872 | tf_op jit(solution)/shard_map/ppermute | solution.py:19
  17.2 4.3 %collective-permute-start.3 = (bf16[2,128,1024]{1,2,0:T(8,128)(2,1)}, bf16[2,128,1024]{1,2,0:T(8,128)(2,1)}, u32[]{:S(2)}, u32[]{:S(2)}) collective-permute-start(bf16[2,128,1024]{1,2,0:T(8,128)(2,1)} %pad_maximum_fusion), channel_id=1, source_target_pairs={{0,4},{4,8},{8,12},{12,16},{16,20},{20,24},{24,28},{1,5},{5,9},{9,... | collective-permute-start | bytes 1572872 | tf_op jit(solution)/shard_map/ppermute | solution.py:19
  21.5 1.1 convert_multiply_fusion
  23.3 2.6 %copy.265 = f32[16,8,8,256]{3,2,1,0:T(8,128)} copy(f32[16,8,8,256]{3,1,2,0:T(8,128)} %bitcast.250) | data formatting | bytes 2097152
  25.9 1.4 %reduce_sum.91 = f32[128,8]{1,0:T(8,128)S(1)} reduce(f32[128,8,256]{2,1,0:T(8,128)} %bitcast.251, f32[]{:T(128)} %constant.12.clone.1), dimensions={2}, to_apply=%region_1.0 | reduce | flops 261120 | bytes 1052676 | tf_op jit(solution)/shard_map/reduce_sum | solution.py:24
  27.9 1.3 %copy.186 = bf16[1,128,2048]{1,2,0:T(8,128)(2,1)S(1)} copy(bf16[1,128,2048]{2,1,0:T(8,128)(2,1)} %param.13) | data formatting | bytes 1048576 | tf_op args[6]
  29.2 1.2 %mul.241 = f32[128,8,256]{2,1,0:T(8,128)} broadcast(f32[128,8]{1,0:T(8,128)S(1)} %copy.185), dimensions={0,1} | broadcast | bytes 1052672 | tf_op jit(solution)/shard_map/mul | solution.py:25
  30.4 2.4 %mul.242 = f32[1,128,2048]{2,1,0:T(8,128)} reshape(f32[128,8,256]{2,1,0:T(8,128)} %mul.241) | data formatting | bytes 2097152 | tf_op jit(solution)/shard_map/mul | solution.py:25
  33.5 1.3 %fusion.69 = (bf16[1,128,1024]{1,2,0:T(8,128)(2,1)S(1)}, bf16[1,128,1024]{1,2,0:T(8,128)(2,1)S(1)}) fusion(bf16[2,128,1024]{1,2,0:T(8,128)(2,1)} %collective-permute-done), kind=kLoop, calls=%fused_computation.125 | loop fusion | bytes 1048576 | tf_op jit(solution)/shard_map/slice | solution.py:68
  35.1 1.1 fusion.70
  37.4 1.2 %multiply_reduce_fusion = (f32[128,4,2]{0,2,1:T(2,128)S(1)}, bf16[128,4,2,256]{0,3,2,1:T(8,128)(2,1)}) fusion(bf16[128,4,2,256]{0,3,2,1:T(8,128)(2,1)S(1)} %bitcast.259, f32[128,4,2,256]{0,3,2,1:T(8,128)S(1)} %convolution_bitcast_fusion, f32[4,256,2,128]{3,1,2,0:T(8,128)S(1)} %fusion.65, bf16[128,4,256,1]{0,2,3,1:T(8,128)(2,1)S(1)} %bitcast.267, ...), kind=kOutput, calls=%fused_computation.57 | convolution fusion | flops 69336064 | bytes 3956736 | tf_op jit(solution)/shard_map/hgqk,khd->qhgd/dot_general | solution.py:90
  40.4 0.9 pad_maximum_fusion.1
  41.2 1.3 %collective-permute-start.4 = (bf16[2,128,4,256]{1,3,2,0:T(8,128)(2,1)}, bf16[2,128,4,256]{1,3,2,0:T(8,128)(2,1)}, u32[]{:S(2)}, u32[]{:S(2)}) collective-permute-start(bf16[2,128,4,256]{1,3,2,0:T(8,128)(2,1)} %pad_maximum_fusion.1), channel_id=1, source_target_pairs={{4,0},{8,4},{12,8},{16,12},{20,16},{24,20},{28,24},{5,1},{9,5},{13... | collective-permute-start | bytes 1572872 | tf_op jit(solution)/shard_map/ppermute | solution.py:19
  42.8 0.9 pad_maximum_fusion.2
  43.7 1.3 %collective-permute-start.5 = (bf16[2,128,4,256]{1,3,2,0:T(8,128)(2,1)}, bf16[2,128,4,256]{1,3,2,0:T(8,128)(2,1)}, u32[]{:S(2)}, u32[]{:S(2)}) collective-permute-start(bf16[2,128,4,256]{1,3,2,0:T(8,128)(2,1)} %pad_maximum_fusion.2), channel_id=1, source_target_pairs={{8,0},{12,4},{16,8},{20,12},{24,16},{28,20},{9,1},{13,5},{17,9},{2... | collective-permute-start | bytes 1572872 | tf_op jit(solution)/shard_map/ppermute | solution.py:19
  45.3 1.5 %fusion.38 = (f32[256]{0:T(256)S(1)}, f32[128,4,2]{0,2,1:T(2,128)S(1)}, f32[4,256,2,128]{3,1,2,0:T(8,128)}) fusion(f32[128,4,2,256]{0,3,2,1:T(8,128)S(1)} %bitcast.249, f32[128,4,2]{0,2,1:T(2,128)S(1)} %bitcast.275, f32[256]{0:T(256)S(1)} %broadcast_multiply_fusion.5, f32[4,256,2,128]{3,1,2,0:T(8,128)S(1)} %fusion.57, f32[4,256,2,128]{3,1,2,0:T(8,128)S(1)} %fusion.72, ...), kind=kOutput, calls=%fused_computation.55 | convolution fusion | flops 69466880 | bytes 4728832 | tf_op jit(solution)/shard_map/hgqk,khd->qhgd/dot_general | solution.py:111
  47.1 1.2 %mul.262 = f32[1,128,2048]{2,1,0:T(8,128)} reshape(f32[128,8,256]{2,1,0:T(8,128)S(1)} %mul.261) | data formatting | bytes 2097152 | tf_op jit(solution)/shard_map/mul | solution.py:31
  48.3 1.3 %broadcast_multiply_fusion = f32[4,256,2,128]{3,1,2,0:T(8,128)S(1)} fusion(f32[4,256,2,128]{3,1,2,0:T(8,128)} %get-tuple-element.59), kind=kLoop, calls=%fused_computation.74 | loop fusion | flops 262144 | bytes 2097152 | tf_op jit(solution)/shard_map/mul | solution.py:126
  49.6 1.3 %copy.196 = f32[1,128,2048]{2,1,0:T(8,128)} copy(f32[1,128,2048]{1,2,0:T(8,128)S(1)} %bitcast.252) | data formatting | bytes 2097152 | tf_op jit(solution)/shard_map/reshape | solution.py:126
  50.9 2.1 %copy.207 = bf16[1,128,2048]{2,1,0:T(8,128)(2,1)} copy(bf16[1,128,2048]{1,2,0:T(8,128)(2,1)} %bitcast.265) | data formatting | bytes 1048576
  53.1 2.7 %multiply_convert_fusion = bf16[1,128,2048]{2,1,0:T(8,128)(2,1)} fusion(f32[1,128,2048]{2,1,0:T(8,128)S(1)} %copy-done.1, f32[1,128,2048]{2,1,0:T(8,128)} %mul.262, f32[1,128,2048]{2,1,0:T(8,128)} %copy.196, bf16[1,128,2048]{2,1,0:T(8,128)(2,1)S(1)} %copy-done, f32[2048]{0:T(1024)S(1)} %bitcast.276), kind=kLoop, calls=%fused_computation.56 | loop fusion | flops 1835008 | bytes 4202496 | tf_op jit(solution)/shard_map/convert_element_type | solution.py:140
  55.8 3.2 %collective-permute-done.4 = bf16[2,128,4,256]{1,3,2,0:T(8,128)(2,1)} collective-permute-done((bf16[2,128,4,256]{1,3,2,0:T(8,128)(2,1)}, bf16[2,128,4,256]{1,3,2,0:T(8,128)(2,1)}, u32[]{:S(2)}, u32[]{:S(2)}) %collective-permute-start.4) | collective-permute-done | bytes 524320 | tf_op jit(solution)/shard_map/ppermute | solution.py:19
  58.9 13.2 %collective-permute-done.5 = bf16[2,128,4,256]{1,3,2,0:T(8,128)(2,1)} collective-permute-done((bf16[2,128,4,256]{1,3,2,0:T(8,128)(2,1)}, bf16[2,128,4,256]{1,3,2,0:T(8,128)(2,1)}, u32[]{:S(2)}, u32[]{:S(2)}) %collective-permute-start.5) | collective-permute-done | bytes 524320 | tf_op jit(solution)/shard_map/ppermute | solution.py:19
  72.1 1.5 %multiply_reduce_fusion.1 = (f32[256]{0:T(256)S(1)}, f32[128,4]{0,1:T(4,128)S(1)}, f32[128,4,256]{0,2,1:T(8,128)S(1)}) fusion(f32[128,4,256]{0,2,1:T(8,128)S(1)} %get-tuple-element.43, f32[128,4]{0,1:T(4,128)S(1)} %add_rsqrt_fusion.1, f32[256]{0:T(256)S(1)} %copy-done.7, bf16[2,128,4,256]{1,3,2,0:T(8,128)(2,1)} %collective-permute-done.5, ...), kind=kOutput, calls=%fused_computation.71 | convolution fusion | flops 68812032 | bytes 2365440 | tf_op jit(solution)/shard_map/hgqk,qhgd->khd/dot_general | solution.py:115
  73.5 38.4 %all-reduce = (f32[256]{0:T(256)S(1)}, f32[256]{0:T(256)S(1)}) all-reduce(f32[256]{0:T(256)S(1)} %get-tuple-element.36, f32[256]{0:T(256)S(1)} %get-tuple-element.38), channel_id=1, replica_groups=mesh['ctx'=8,'dp'=4] {'ctx','dp'}, use_global_device_ids=true, to_apply=%region_9.10 | all-reduce | flops 512 | bytes 4096 | tf_op jit(solution)/shard_map/psum | solution.py:153
  113.0 1.3 %fusion.39 = bf16[128,4,256]{0,2,1:T(8,128)(2,1)S(1)} fusion(bf16[2,128,4,256]{1,3,2,0:T(8,128)(2,1)} %collective-permute-done.5, bf16[2,128,4,256]{1,3,2,0:T(8,128)(2,1)} %collective-permute-done.4, bf16[128,4,2,256]{0,3,2,1:T(8,128)(2,1)S(1)} %bitcast.264, f32[4,2,128,128]{2,3,1,0:T(8,128)S(1)} %copy-done.4, f32[4,2,128]{2,1,0:T(2,128)S(1)} %bitcast.290), kind=kOutput, calls=%fused_computation.63 | convolution fusion | flops 68288512 | bytes 1839104 | tf_op jit(solution)/shard_map/hgqk,qhgd->khd/dot_general | solution.py:120
  114.4 0.8 copy.209
  115.4 0.8 copy.208
  (66 shorter events, 9.3 us)
Async XLA Ops:
  0.6 0.7 copy-start.9
  1.3 31.5 %collective-permute-start.1 = (s32[128]{0:T(128)S(1)}, s32[128]{0:T(128)S(1)}, u32[]{:S(2)}, u32[]{:S(2)}) collective-permute-start(s32[128]{0:T(128)S(1)} %bitcast.294), channel_id=1, source_target_pairs={{0,8},{4,12},{8,16},{12,20},{16,24},{20,28},{1,9},{5,13},{9,17},{1... | collective-permute-start | bytes 1544 | tf_op jit(solution)/shard_map/ppermute | solution.py:19
  6.2 26.6 %collective-permute-start.2 = (s32[128]{0:T(128)S(1)}, s32[128]{0:T(128)S(1)}, u32[]{:S(2)}, u32[]{:S(2)}) collective-permute-start(s32[128]{0:T(128)S(1)} %bitcast.295), channel_id=1, source_target_pairs={{0,4},{4,8},{8,12},{12,16},{16,20},{20,24},{24,28},{1,5},{5,9},{9,... | collective-permute-start | bytes 1544 | tf_op jit(solution)/shard_map/ppermute | solution.py:19
  10.7 1.0 copy-start.2
  10.8 0.7 copy-start.7
  12.1 9.4 %copy-start = (bf16[1,128,2048]{2,1,0:T(8,128)(2,1)S(1)}, bf16[1,128,2048]{2,1,0:T(8,128)(2,1)}, u32[]{:S(2)}) copy-start(bf16[1,128,2048]{2,1,0:T(8,128)(2,1)} %param.7) | copy-start | bytes 1572868
  12.9 20.5 %collective-permute-start = (bf16[2,128,1024]{1,2,0:T(8,128)(2,1)}, bf16[2,128,1024]{1,2,0:T(8,128)(2,1)}, u32[]{:S(2)}, u32[]{:S(2)}) collective-permute-start(bf16[2,128,1024]{1,2,0:T(8,128)(2,1)} %pad_maximum_fusion), channel_id=1, source_target_pairs={{0,8},{4,12},{8,16},{12,20},{16,24},{20,28},{1,9},{5,13},{9,17},{1... | collective-permute-start | bytes 1572872 | tf_op jit(solution)/shard_map/ppermute | solution.py:19
  17.2 17.8 %collective-permute-start.3 = (bf16[2,128,1024]{1,2,0:T(8,128)(2,1)}, bf16[2,128,1024]{1,2,0:T(8,128)(2,1)}, u32[]{:S(2)}, u32[]{:S(2)}) collective-permute-start(bf16[2,128,1024]{1,2,0:T(8,128)(2,1)} %pad_maximum_fusion), channel_id=1, source_target_pairs={{0,4},{4,8},{8,12},{12,16},{16,20},{20,24},{24,28},{1,5},{5,9},{9,... | collective-permute-start | bytes 1572872 | tf_op jit(solution)/shard_map/ppermute | solution.py:19
  22.6 0.7 copy-start.8
  33.5 6.0 %copy-start.3 = (f32[4,2,128,128]{2,3,1,0:T(8,128)}, f32[4,2,128,128]{2,3,1,0:T(8,128)S(1)}, u32[]{:S(2)}) copy-start(f32[4,2,128,128]{2,3,1,0:T(8,128)S(1)} %get-tuple-element.52) | copy-start | bytes 1572868
  39.8 5.2 %copy-start.5 = (bf16[4,2,128,128]{2,3,1,0:T(8,128)(2,1)}, bf16[4,2,128,128]{2,3,1,0:T(8,128)(2,1)S(1)}, u32[]{:S(2)}) copy-start(bf16[4,2,128,128]{2,3,1,0:T(8,128)(2,1)S(1)} %fusion.20) | copy-start | bytes 786436
  41.2 17.7 %collective-permute-start.4 = (bf16[2,128,4,256]{1,3,2,0:T(8,128)(2,1)}, bf16[2,128,4,256]{1,3,2,0:T(8,128)(2,1)}, u32[]{:S(2)}, u32[]{:S(2)}) collective-permute-start(bf16[2,128,4,256]{1,3,2,0:T(8,128)(2,1)} %pad_maximum_fusion.1), channel_id=1, source_target_pairs={{4,0},{8,4},{12,8},{16,12},{20,16},{24,20},{28,24},{5,1},{9,5},{13... | collective-permute-start | bytes 1572872 | tf_op jit(solution)/shard_map/ppermute | solution.py:19
  43.7 28.4 %collective-permute-start.5 = (bf16[2,128,4,256]{1,3,2,0:T(8,128)(2,1)}, bf16[2,128,4,256]{1,3,2,0:T(8,128)(2,1)}, u32[]{:S(2)}, u32[]{:S(2)}) collective-permute-start(bf16[2,128,4,256]{1,3,2,0:T(8,128)(2,1)} %pad_maximum_fusion.2), channel_id=1, source_target_pairs={{8,0},{12,4},{16,8},{20,12},{24,16},{28,20},{9,1},{13,5},{17,9},{2... | collective-permute-start | bytes 1572872 | tf_op jit(solution)/shard_map/ppermute | solution.py:19
  50.9 2.1 %copy-start.1 = (f32[1,128,2048]{2,1,0:T(8,128)S(1)}, f32[1,128,2048]{2,1,0:T(8,128)}, u32[]{:S(2)}) copy-start(f32[1,128,2048]{2,1,0:T(8,128)} %mul.242) | copy-start | bytes 3145732
  53.1 19.0 %copy-start.6 = (bf16[4,2,128,128]{2,3,1,0:T(8,128)(2,1)S(1)}, bf16[4,2,128,128]{2,3,1,0:T(8,128)(2,1)}, u32[]{:S(2)}) copy-start(bf16[4,2,128,128]{2,3,1,0:T(8,128)(2,1)} %copy-done.5) | copy-start | bytes 786436
  55.8 57.3 %copy-start.4 = (f32[4,2,128,128]{2,3,1,0:T(8,128)S(1)}, f32[4,2,128,128]{2,3,1,0:T(8,128)}, u32[]{:S(2)}) copy-start(f32[4,2,128,128]{2,3,1,0:T(8,128)} %copy-done.3) | copy-start | bytes 1572868
where the time goes:
time: 117 us; the launch traced here: 116 us
  blocking collectives  38.4 us (33%)
  local copies, waits for them, and re-layouts  20.3 us (17%)
  starting transfers between devices  19.4 us (17%)
  waiting for transfers between devices  16.3 us (14%)
  other arithmetic  11.1 us (9%)
  matrix products  9.73 us (8%)
    psum x1, blocking collectives, body(): q_total, k_total = lax.psum((q_sum_part, k_sum_part), ('ctx', 'dp'))  38.4 us
    ppermute x6, starting transfers between devices, shifted(): return lax.ppermute(value, axis, pairs)  19.4 us
    ppermute x6, waiting for transfers between devices, shifted(): return lax.ppermute(value, axis, pairs)  16.3 us
    unnamed x31, local copies, waits for them, and re-layouts  11 us
    mul x2, local copies, waits for them, and re-layouts, rms_normalize(): normed = as_float * inv_rms  3.61 us
    convert_element_type x1, other arithmetic, body(): grad_queries = rms_norm_backward(q_grad_norm, q_normed, q_inv, q_gain).as...  2.69 us
  transfers between devices with their start and end apart: 6, of which 2 were waited for; matrix products, arithmetic and copies ran while one was open for 24% of the time, Pallas kernels for 0%

commit v1 on v0

v1 whole, which is shorter than its diff:
```python
import functools

import jax
import jax.numpy as jnp
from jax import lax
from jax.experimental import pallas as pl
from jax.experimental.pallas import tpu as pltpu
from jax.sharding import PartitionSpec as P

HEADS = 8
KV = 4
D = 256
WINDOW = 256
HALO = 2
EPS = 1e-06
SCALE = D ** (-0.5)
MESH = pl.DeviceIdType.MESH
F32 = jnp.float32
BF16 = jnp.bfloat16


def dot(a, b, contract):
    return lax.dot_general(a, b, ((contract[:1], contract[1:]), ((), ())), preferred_element_type=F32)


def hat(x):
    x = x.astype(F32)
    inv = lax.rsqrt(jnp.mean(x * x, -1, keepdims=True) + EPS)
    return x * inv, inv


def norm_backward(up, normed, inv, gain):
    g = up * gain
    return inv * (g - normed * jnp.mean(g * normed, -1, keepdims=True))


def kernel(
    nc, nd,
    q_ref, k_ref, v_ref, qg_ref, kg_ref, seg_ref, do_ref,
    o_ref, dq_ref, dk_ref, dv_ref, gq_ref, gk_ref,
    kvbuf, segbuf, gbuf, grecv, own, part_c, part_d, stage_c, stage_d,
    kv_send, kv_recv, seg_send, seg_recv, g_send, g_recv, r_send, r_recv,
):
    T = k_ref.shape[1]
    me = lax.axis_index("ctx")
    dpi = lax.axis_index("dp")

    barrier = pltpu.get_barrier_semaphore()

    @pl.loop(1, nc)
    def _(d):
        pl.semaphore_signal(barrier, inc=1, device_id={"ctx": lax.rem(me + d, nc)}, device_id_type=MESH)

    @pl.loop(1, nd)
    def _(d):
        pl.semaphore_signal(barrier, inc=1, device_id={"dp": lax.rem(dpi + d, nd)}, device_id_type=MESH)

    def remote(src, dst, send, recv, peer):
        return pltpu.make_async_remote_copy(
            src_ref=src, dst_ref=dst, send_sem=send, recv_sem=recv,
            device_id=peer, device_id_type=MESH,
        )

    def rows(block):
        return pl.ds(block * T, T)

    def kv_copy(g, off):
        return remote(
            kvbuf.at[g, rows(HALO)], kvbuf.at[g, rows(HALO - off)],
            kv_send.at[off - 1, g], kv_recv.at[off - 1, g], {"ctx": me + off},
        )

    def seg_copy(off):
        return remote(
            segbuf.at[HALO], segbuf.at[HALO - off],
            seg_send.at[off - 1], seg_recv.at[off - 1], {"ctx": me + off},
        )

    def grad_copy(g, off):
        return remote(
            gbuf.at[g, rows(HALO - off)], grecv.at[off - 1, g],
            g_send.at[off - 1, g], g_recv.at[off - 1, g], {"ctx": me - off},
        )

    q_gain = qg_ref[...]
    k_gain = kg_ref[...]
    for g in range(KV):
        col = pl.ds(g * D, D)
        kvbuf[g, rows(HALO), 0:D] = (hat(k_ref[0, :, col])[0] * k_gain).astype(BF16)
        kvbuf[g, rows(HALO), D:] = v_ref[0, :, col]
    seg_row = seg_ref[...]
    segbuf[HALO] = jnp.broadcast_to(seg_row, (8, T))

    pl.semaphore_wait(barrier, nc - 1 + nd - 1)

    for off in range(1, HALO + 1):
        @pl.when(me + off < nc)
        def _(off=off):
            seg_copy(off).start()

    for g in range(KV):
        for off in range(1, HALO + 1):
            @pl.when(me + off < nc)
            def _(off=off, g=g):
                kv_copy(g, off).start()

    for off in range(1, HALO + 1):
        @pl.when(me < off)
        def _(off=off):
            for g in range(KV):
                kvbuf[g, rows(HALO - off)] = jnp.zeros((T, 2 * D), BF16)
            segbuf[HALO - off] = jnp.full((8, T), -1, jnp.int32)

        @pl.when(me + off >= nc)
        def _(off=off):
            for g in range(KV):
                grecv[off - 1, g] = jnp.zeros((T, 2 * D), BF16)

    qs = []
    for h in range(HEADS):
        q_hat, _ = hat(q_ref[0, :, pl.ds(h * D, D)])
        qs.append((q_hat * q_gain).astype(BF16) * jnp.asarray(SCALE, BF16))

    seg_q = jnp.broadcast_to(seg_row, (T, T)).T
    for off in range(1, HALO + 1):
        @pl.when(me >= off)
        def _(off=off):
            seg_copy(off).wait_recv()
    qi = lax.broadcasted_iota(jnp.int32, (T, T), 0)
    ki = lax.broadcasted_iota(jnp.int32, (T, T), 1)
    masks = []
    for block in range(HALO + 1):
        dist = qi - ki + (HALO - block) * T
        same = seg_q == jnp.broadcast_to(segbuf[block, 0:1, :], (T, T))
        masks.append((dist >= 0) & (dist < WINDOW) & same)
    mask = jnp.concatenate(masks, 1)
    mask = jnp.concatenate([mask, mask], 0)

    gq = jnp.zeros((1, D), F32)
    gk = jnp.zeros((1, D), F32)
    for g in range(KV):
        for off in range(1, HALO + 1):
            @pl.when(me >= off)
            def _(off=off, g=g):
                kv_copy(g, off).wait_recv()
        K = kvbuf[g, :, 0:D]
        V = kvbuf[g, :, D:]
        Q = jnp.concatenate([qs[2 * g], qs[2 * g + 1]], 0)
        dO = jnp.concatenate(
            [do_ref[0, :, pl.ds(2 * g * D, D)], do_ref[0, :, pl.ds((2 * g + 1) * D, D)]], 0
        )
        E = jnp.where(mask, jnp.exp(dot(Q, K, (1, 1))), 0.0)
        prob = E * (1.0 / jnp.sum(E, -1, keepdims=True))
        prob_b = prob.astype(BF16)
        out = dot(prob_b, V, (1, 0)).astype(BF16)
        for i in range(2):
            o_ref[0, :, pl.ds((2 * g + i) * D, D)] = out[i * T:(i + 1) * T]
        delta = jnp.sum(dO.astype(F32) * out.astype(F32), -1, keepdims=True)
        ds = (prob * (dot(dO, V, (1, 1)) - delta)).astype(BF16)
        dK = dot(ds, Q, (0, 0))
        dV = dot(prob_b, dO, (0, 0))
        gbuf[g, :, 0:D] = dK[:HALO * T].astype(BF16)
        gbuf[g, :, D:] = dV[:HALO * T].astype(BF16)
        for off in range(1, HALO + 1):
            @pl.when(me >= off)
            def _(off=off, g=g):
                grad_copy(g, off).start()
        own[g, :, 0:D] = dK[HALO * T:]
        own[g, :, D:] = dV[HALO * T:]
        gk += jnp.sum(dK * K.astype(F32), 0, keepdims=True)
        dQ = dot(ds, K, (1, 0)) * SCALE
        for i in range(2):
            col = pl.ds((2 * g + i) * D, D)
            q_hat, q_inv = hat(q_ref[0, :, col])
            up = dQ[i * T:(i + 1) * T]
            gq += jnp.sum(up * q_hat, 0, keepdims=True)
            dq_ref[0, :, col] = norm_backward(up, q_hat, q_inv, q_gain).astype(BF16)

    def reduce_over(axis, count, index, part, stage, which):
        def one(d):
            return remote(
                part, stage.at[d - 1], r_send.at[which], r_recv.at[which],
                {axis: lax.rem(index + d, count)},
            )

        @pl.loop(1, count)
        def _(d):
            one(d).start()

        pltpu.make_async_copy(stage, stage, r_recv.at[which]).wait()
        return part[...] + jnp.sum(stage[...], 0)

    part_c[0:1, :] = gq
    part_c[1:2, :] = gk / k_gain
    part_d[...] = reduce_over("ctx", nc, me, part_c, stage_c, 0)
    total = reduce_over("dp", nd, dpi, part_d, stage_d, 1) * float(nc * nd * T) ** (-0.5)
    gq_ref[...] = total[0:1]
    gk_ref[...] = total[1:2]

    for g in range(KV):
        for off in range(1, HALO + 1):
            @pl.when(me + off < nc)
            def _(off=off, g=g):
                grad_copy(g, off).wait_recv()
        col = pl.ds(g * D, D)
        acc = own[g] + grecv[0, g].astype(F32) + grecv[1, g].astype(F32)
        k_hat, k_inv = hat(k_ref[0, :, col])
        dk_ref[0, :, col] = norm_backward(acc[:, 0:D], k_hat, k_inv, k_gain).astype(BF16)
        dv_ref[0, :, col] = acc[:, D:].astype(BF16)

    for off in range(1, HALO + 1):
        @pl.when(me + off < nc)
        def _(off=off):
            seg_copy(off).wait_send()
            for g in range(KV):
                kv_copy(g, off).wait_send()

        @pl.when(me >= off)
        def _(off=off):
            for g in range(KV):
                grad_copy(g, off).wait_send()
    pltpu.make_async_copy(stage_c, stage_c, r_send.at[0]).wait()
    pltpu.make_async_copy(stage_d, stage_d, r_send.at[1]).wait()


def body(nc, nd, queries, keys, values, q_gain, key_norm_gain, segment_ids, output_gradient):
    T = queries.shape[1]
    dma = pltpu.SemaphoreType.DMA
    vmem = pl.BlockSpec(memory_space=pltpu.VMEM)
    outs = pl.pallas_call(
        functools.partial(kernel, nc, nd),
        out_shape=(
            jax.ShapeDtypeStruct(queries.shape, BF16),
            jax.ShapeDtypeStruct(queries.shape, BF16),
            jax.ShapeDtypeStruct(keys.shape, BF16),
            jax.ShapeDtypeStruct(values.shape, BF16),
            jax.ShapeDtypeStruct((1, D), F32),
            jax.ShapeDtypeStruct((1, D), F32),
        ),
        in_specs=[vmem] * 7,
        out_specs=(vmem,) * 6,
        scratch_shapes=[
            pltpu.VMEM((KV, (HALO + 1) * T, 2 * D), BF16),
            pltpu.VMEM((HALO + 1, 8, T), jnp.int32),
            pltpu.VMEM((KV, HALO * T, 2 * D), BF16),
            pltpu.VMEM((HALO, KV, T, 2 * D), BF16),
            pltpu.VMEM((KV, T, 2 * D), F32),
            pltpu.VMEM((2, D), F32),
            pltpu.VMEM((2, D), F32),
            pltpu.VMEM((nc - 1, 2, D), F32),
            pltpu.VMEM((nd - 1, 2, D), F32),
            dma((HALO, KV)), dma((HALO, KV)),
            dma((HALO,)), dma((HALO,)),
            dma((HALO, KV)), dma((HALO, KV)),
            dma((2,)), dma((2,)),
        ],
        compiler_params=pltpu.CompilerParams(
            collective_id=0, has_side_effects=True, vmem_limit_bytes=48 * 1024 * 1024,
        ),
    )(queries, keys, values, q_gain.reshape(1, D), key_norm_gain.reshape(1, D), segment_ids, output_gradient)
    attn_out, dq, dk, dv, gq, gk = outs
    return attn_out, dq, dk, dv, gq.reshape(D), gk.reshape(D)


def solution(mesh):
    tokens = P("dp", "ctx", None)
    return jax.shard_map(
        functools.partial(body, mesh.shape["ctx"], mesh.shape["dp"]),
        mesh=mesh,
        in_specs=(tokens, tokens, tokens, P(), P(), P("dp", "ctx"), tokens),
        out_specs=(tokens, tokens, tokens, tokens, P(), P()),
        check_vma=False,
    )
```

time: 117 us -> 49.3 us (0.42)
  Pallas kernels: 0 us -> 39.6 us
  blocking collectives: 38.4 us -> 0 us
  starting transfers between devices: 19.4 us -> 0 us
  waiting for transfers between devices: 16.3 us -> 0 us
  local copies, waits for them, and re-layouts: 20.3 us -> 8.77 us
  other arithmetic: 11.1 us -> 0 us
  matrix products: 9.73 us -> 0 us
    pallas_call x0 -> x1, Pallas kernels: none -> 39.6 us  [body(): pl.pallas_call(functools.partial(kernel, nc, nd), out_shape=(jax.ShapeDty...]
    psum x1 -> x0, blocking collectives: 38.4 us -> none  [body(): q_total, k_total = lax.psum((q_sum_part, k_sum_part), ('ctx', 'dp'))]
    ppermute x6 -> x0, starting transfers between devices: 19.4 us -> none  [shifted(): return lax.ppermute(value, axis, pairs)]
    ppermute x6 -> x0, waiting for transfers between devices: 16.3 us -> none  [shifted(): return lax.ppermute(value, axis, pairs)]
    dot_general x18 -> x0, matrix products: 9.73 us -> none  [the longest x3 2.09 us: backward_block(): jnp.einsum('hgqk,khd->qhgd', score_grad, key_block_list[block], preferred...]
    mul x4 -> x0, local copies, waits for them, and re-layouts: 5 us -> none  [the longest x2 3.61 us: rms_normalize(): normed = as_float * inv_rms]
    mul x5 -> x0, other arithmetic: 3.53 us -> none  [the longest x1 1.3 us: body(): sum((item[0] for item in back_blocks)) * score_scale]
    convert_element_type x4 -> x0, other arithmetic: 3.23 us -> none  [the longest x1 2.69 us: body(): grad_queries = rms_norm_backward(q_grad_norm, q_normed, q_inv, q_gain).as...]
  transfers between devices with their start and end apart: 6 -> 0, of which waited for: 2 -> 0; matrix products, arithmetic and copies ran while one was open for 24% -> 0% of each run, Pallas kernels for 0% -> 0%
where the time goes in v1:
time: 49.3 us; the launch traced here: 49 us
  Pallas kernels  39.6 us (80%)
  local copies, waits for them, and re-layouts  8.77 us (18%)
  between operations  0.67 us (1%)
    pallas_call x1, Pallas kernels, body(): pl.pallas_call(functools.partial(kernel, nc, nd), out_shape=(jax.ShapeDty...  39.6 us
    unnamed x20, local copies, waits for them, and re-layouts  8.77 us

profile of v1, /device:TPU:0, one launch (start us, length us, event | category | flops | bytes accessed | tf_op | source)
XLA Modules:
  0.0 49.0 jit_solution(14735366831292462597)
XLA Ops:
  0.6 0.0 copy-start.5
  0.6 0.0 copy-start.4
  0.7 0.0 copy-start.6
  0.7 0.7 %copy-done.5 = f32[256]{0:T(256)S(1)} copy-done((f32[256]{0:T(256)S(1)}, f32[256]{0:T(256)}, u32[]{:S(2)}) %copy-start.5) | copy-done | bytes 1048
  1.3 0.0 copy-done.4
  1.3 0.0 copy-done.6
  1.3 0.0 copy-start
  1.3 1.0 %copy-done = bf16[1,128,2048]{2,1,0:T(8,128)(2,1)S(1)} copy-done((bf16[1,128,2048]{2,1,0:T(8,128)(2,1)S(1)}, bf16[1,128,2048]{2,1,0:T(8,128)(2,1)}, u32[]{:S(2)}) %copy-start) | copy-done | bytes 524312
  2.4 0.0 copy-start.1
  2.4 1.0 %copy-done.1 = bf16[1,128,2048]{2,1,0:T(8,128)(2,1)S(1)} copy-done((bf16[1,128,2048]{2,1,0:T(8,128)(2,1)S(1)}, bf16[1,128,2048]{2,1,0:T(8,128)(2,1)}, u32[]{:S(2)}) %copy-start.1) | copy-done | bytes 524312
  3.4 0.0 copy-start.2
  3.4 0.9 %copy-done.2 = bf16[1,128,1024]{2,1,0:T(8,128)(2,1)S(1)} copy-done((bf16[1,128,1024]{2,1,0:T(8,128)(2,1)S(1)}, bf16[1,128,1024]{2,1,0:T(8,128)(2,1)}, u32[]{:S(2)}) %copy-start.2) | copy-done | bytes 262168
  4.4 0.0 copy-start.3
  4.4 0.9 %copy-done.3 = bf16[1,128,1024]{2,1,0:T(8,128)(2,1)S(1)} copy-done((bf16[1,128,1024]{2,1,0:T(8,128)(2,1)S(1)}, bf16[1,128,1024]{2,1,0:T(8,128)(2,1)}, u32[]{:S(2)}) %copy-start.3) | copy-done | bytes 262168
  5.3 39.6 %shard_map.118 = (bf16[1,128,2048]{2,1,0:T(8,128)(2,1)S(1)}, bf16[1,128,2048]{2,1,0:T(8,128)(2,1)S(1)}, bf16[1,128,1024]{2,1,0:T(8,128)(2,1)S(1)}, bf16[1,128,10...) custom-call(bf16[1,128,2048]{2,1,0:T(8,128)(2,1)S(1)} %copy-done, ...), custom_call_target="tpu_custom_call" | custom-call | tf_op jit(solution)/shard_map/pallas_call | solution.py:230
  44.9 0.8 %copy.19 = bf16[1,128,2048]{2,1,0:T(8,128)(2,1)} copy(bf16[1,128,2048]{2,1,0:T(8,128)(2,1)S(1)} %get-tuple-element.24) | data formatting | bytes 1048576
  45.7 0.8 %copy.20 = bf16[1,128,2048]{2,1,0:T(8,128)(2,1)} copy(bf16[1,128,2048]{2,1,0:T(8,128)(2,1)S(1)} %get-tuple-element.25) | data formatting | bytes 1048576
  46.5 0.7 %copy.21 = bf16[1,128,1024]{2,1,0:T(8,128)(2,1)} copy(bf16[1,128,1024]{2,1,0:T(8,128)(2,1)S(1)} %get-tuple-element.26) | data formatting | bytes 524288
  47.2 0.7 %copy.22 = bf16[1,128,1024]{2,1,0:T(8,128)(2,1)} copy(bf16[1,128,1024]{2,1,0:T(8,128)(2,1)S(1)} %get-tuple-element.27) | data formatting | bytes 524288
  47.9 0.6 %copy.23 = f32[256]{0:T(256)} copy(f32[256]{0:T(256)S(1)} %bitcast.5) | data formatting | bytes 2048
  48.4 0.6 %copy.24 = f32[256]{0:T(256)} copy(f32[256]{0:T(256)S(1)} %bitcast.4) | data formatting | bytes 2048
Async XLA Ops:
  0.6 0.7 %copy-start.5 = (f32[256]{0:T(256)S(1)}, f32[256]{0:T(256)}, u32[]{:S(2)}) copy-start(f32[256]{0:T(256)} %param.11) | copy-start | bytes 3076
  0.6 0.7 %copy-start.4 = (f32[256]{0:T(256)S(1)}, f32[256]{0:T(256)}, u32[]{:S(2)}) copy-start(f32[256]{0:T(256)} %param.10) | copy-start | bytes 3076
  0.7 0.7 %copy-start.6 = (s32[1,128]{1,0:T(1,128)S(1)}, s32[1,128]{1,0:T(1,128)}, u32[]{:S(2)}) copy-start(s32[1,128]{1,0:T(1,128)} %seg_ref.1) | copy-start | bytes 1540
  1.3 1.0 %copy-start = (bf16[1,128,2048]{2,1,0:T(8,128)(2,1)S(1)}, bf16[1,128,2048]{2,1,0:T(8,128)(2,1)}, u32[]{:S(2)}) copy-start(bf16[1,128,2048]{2,1,0:T(8,128)(2,1)} %q_ref.1) | copy-start | bytes 1572868
  2.4 1.0 %copy-start.1 = (bf16[1,128,2048]{2,1,0:T(8,128)(2,1)S(1)}, bf16[1,128,2048]{2,1,0:T(8,128)(2,1)}, u32[]{:S(2)}) copy-start(bf16[1,128,2048]{2,1,0:T(8,128)(2,1)} %do_ref.1) | copy-start | bytes 1572868
  3.4 0.9 %copy-start.2 = (bf16[1,128,1024]{2,1,0:T(8,128)(2,1)S(1)}, bf16[1,128,1024]{2,1,0:T(8,128)(2,1)}, u32[]{:S(2)}) copy-start(bf16[1,128,1024]{2,1,0:T(8,128)(2,1)} %k_ref.1) | copy-start | bytes 786436
  4.4 0.9 %copy-start.3 = (bf16[1,128,1024]{2,1,0:T(8,128)(2,1)S(1)}, bf16[1,128,1024]{2,1,0:T(8,128)(2,1)}, u32[]{:S(2)}) copy-start(bf16[1,128,1024]{2,1,0:T(8,128)(2,1)} %v_ref.1) | copy-start | bytes 786436

commit v2 on v1

--- a/solution.py
+++ b/solution.py
@@ -36,24 +36,53 @@
 
 def kernel(
     nc, nd,
-    q_ref, k_ref, v_ref, qg_ref, kg_ref, seg_ref, do_ref,
-    o_ref, dq_ref, dk_ref, dv_ref, gq_ref, gk_ref,
-    kvbuf, segbuf, gbuf, grecv, own, part_c, part_d, stage_c, stage_d,
+    q_hbm, k_hbm, v_hbm, qg_hbm, kg_hbm, seg_hbm, do_hbm,
+    o_hbm, dq_hbm, dk_hbm, dv_hbm, gq_hbm, gk_hbm,
+    q_ref, k_ref, do_ref, qg_ref, kg_ref, seg_ref, in_sem,
+    o_ref, dq_ref, dk_ref, dv_ref, gq_ref, gk_ref, out_sem, gain_sem,
+    kvbuf, segbuf, gbuf, grecv, own, part, stage,
     kv_send, kv_recv, seg_send, seg_recv, g_send, g_recv, r_send, r_recv,
 ):
-    T = k_ref.shape[1]
+    T = k_hbm.shape[1]
     me = lax.axis_index("ctx")
     dpi = lax.axis_index("dp")
 
+    loads = {}
+
+    def load(name, src, dst):
+        loads[name] = pltpu.make_async_copy(src, dst, in_sem.at[len(loads)])
+        loads[name].start()
+
+    stores = []
+
+    def store(src, dst, sem):
+        stores.append(pltpu.make_async_copy(src, dst, sem))
+        stores[-1].start()
+
+    def arrive(name):
+        loads[name].wait()
+
+    load("kg", kg_hbm, kg_ref)
+    for g in range(KV):
+        col = pl.ds(g * D, D)
+        load(f"k{g}", k_hbm.at[0, :, col], k_ref.at[:, col])
+        load(f"v{g}", v_hbm.at[0, :, col], kvbuf.at[g, pl.ds(HALO * T, T), pl.ds(D, D)])
+    load("seg", seg_hbm, seg_ref)
+    load("qg", qg_hbm, qg_ref)
+    load("q", q_hbm.at[0], q_ref)
+    load("do", do_hbm.at[0], do_ref)
+
     barrier = pltpu.get_barrier_semaphore()
 
-    @pl.loop(1, nc)
+    rank = me * nd + dpi
+
+    def peer_of(d):
+        other = lax.rem(rank + d, nc * nd)
+        return {"ctx": other // nd, "dp": lax.rem(other, nd)}
+
+    @pl.loop(1, nc * nd)
     def _(d):
-        pl.semaphore_signal(barrier, inc=1, device_id={"ctx": lax.rem(me + d, nc)}, device_id_type=MESH)
-
-    @pl.loop(1, nd)
-    def _(d):
-        pl.semaphore_signal(barrier, inc=1, device_id={"dp": lax.rem(dpi + d, nd)}, device_id_type=MESH)
+        pl.semaphore_signal(barrier, inc=1, device_id=peer_of(d), device_id_type=MESH)
 
     def remote(src, dst, send, recv, peer):
         return pltpu.make_async_remote_copy(
@@ -76,29 +105,31 @@
             seg_send.at[off - 1], seg_recv.at[off - 1], {"ctx": me + off},
         )
 
+    def sum_copy(d):
+        return remote(part, stage.at[d - 1], r_send, r_recv, peer_of(d))
+
     def grad_copy(g, off):
         return remote(
             gbuf.at[g, rows(HALO - off)], grecv.at[off - 1, g],
             g_send.at[off - 1, g], g_recv.at[off - 1, g], {"ctx": me - off},
         )
 
-    q_gain = qg_ref[...]
+    arrive("kg")
     k_gain = kg_ref[...]
     for g in range(KV):
         col = pl.ds(g * D, D)
-        kvbuf[g, rows(HALO), 0:D] = (hat(k_ref[0, :, col])[0] * k_gain).astype(BF16)
-        kvbuf[g, rows(HALO), D:] = v_ref[0, :, col]
-    seg_row = seg_ref[...]
-    segbuf[HALO] = jnp.broadcast_to(seg_row, (8, T))
-
-    pl.semaphore_wait(barrier, nc - 1 + nd - 1)
-
-    for off in range(1, HALO + 1):
-        @pl.when(me + off < nc)
-        def _(off=off):
-            seg_copy(off).start()
-
-    for g in range(KV):
+        arrive(f"k{g}")
+        kvbuf[g, rows(HALO), 0:D] = (hat(k_ref[:, col])[0] * k_gain).astype(BF16)
+        arrive(f"v{g}")
+        if g == 0:
+            arrive("seg")
+            seg_row = seg_ref[...]
+            segbuf[HALO] = jnp.broadcast_to(seg_row, (8, T))
+            pl.semaphore_wait(barrier, nc * nd - 1)
+            for off in range(1, HALO + 1):
+                @pl.when(me + off < nc)
+                def _(off=off):
+                    seg_copy(off).start()
         for off in range(1, HALO + 1):
             @pl.when(me + off < nc)
             def _(off=off, g=g):
@@ -116,9 +147,12 @@
             for g in range(KV):
                 grecv[off - 1, g] = jnp.zeros((T, 2 * D), BF16)
 
+    arrive("qg")
+    q_gain = qg_ref[...]
+    arrive("q")
     qs = []
     for h in range(HEADS):
-        q_hat, _ = hat(q_ref[0, :, pl.ds(h * D, D)])
+        q_hat, _ = hat(q_ref[:, pl.ds(h * D, D)])
         qs.append((q_hat * q_gain).astype(BF16) * jnp.asarray(SCALE, BF16))
 
     seg_q = jnp.broadcast_to(seg_row, (T, T)).T
@@ -136,6 +170,7 @@
     mask = jnp.concatenate(masks, 1)
     mask = jnp.concatenate([mask, mask], 0)
 
+    arrive("do")
     gq = jnp.zeros((1, D), F32)
     gk = jnp.zeros((1, D), F32)
     for g in range(KV):
@@ -147,14 +182,14 @@
         V = kvbuf[g, :, D:]
         Q = jnp.concatenate([qs[2 * g], qs[2 * g + 1]], 0)
         dO = jnp.concatenate(
-            [do_ref[0, :, pl.ds(2 * g * D, D)], do_ref[0, :, pl.ds((2 * g + 1) * D, D)]], 0
+            [do_ref[:, pl.ds(2 * g * D, D)], do_ref[:, pl.ds((2 * g + 1) * D, D)]], 0
         )
         E = jnp.where(mask, jnp.exp(dot(Q, K, (1, 1))), 0.0)
         prob = E * (1.0 / jnp.sum(E, -1, keepdims=True))
         prob_b = prob.astype(BF16)
         out = dot(prob_b, V, (1, 0)).astype(BF16)
         for i in range(2):
-            o_ref[0, :, pl.ds((2 * g + i) * D, D)] = out[i * T:(i + 1) * T]
+            o_ref[:, pl.ds((2 * g + i) * D, D)] = out[i * T:(i + 1) * T]
         delta = jnp.sum(dO.astype(F32) * out.astype(F32), -1, keepdims=True)
         ds = (prob * (dot(dO, V, (1, 1)) - delta)).astype(BF16)
         dK = dot(ds, Q, (0, 0))
@@ -171,31 +206,20 @@
         dQ = dot(ds, K, (1, 0)) * SCALE
         for i in range(2):
             col = pl.ds((2 * g + i) * D, D)
-            q_hat, q_inv = hat(q_ref[0, :, col])
+            q_hat, q_inv = hat(q_ref[:, col])
             up = dQ[i * T:(i + 1) * T]
             gq += jnp.sum(up * q_hat, 0, keepdims=True)
-            dq_ref[0, :, col] = norm_backward(up, q_hat, q_inv, q_gain).astype(BF16)
-
-    def reduce_over(axis, count, index, part, stage, which):
-        def one(d):
-            return remote(
-                part, stage.at[d - 1], r_send.at[which], r_recv.at[which],
-                {axis: lax.rem(index + d, count)},
-            )
-
-        @pl.loop(1, count)
-        def _(d):
-            one(d).start()
-
-        pltpu.make_async_copy(stage, stage, r_recv.at[which]).wait()
-        return part[...] + jnp.sum(stage[...], 0)
-
-    part_c[0:1, :] = gq
-    part_c[1:2, :] = gk / k_gain
-    part_d[...] = reduce_over("ctx", nc, me, part_c, stage_c, 0)
-    total = reduce_over("dp", nd, dpi, part_d, stage_d, 1) * float(nc * nd * T) ** (-0.5)
-    gq_ref[...] = total[0:1]
-    gk_ref[...] = total[1:2]
+            dq_ref[:, col] = norm_backward(up, q_hat, q_inv, q_gain).astype(BF16)
+        pair = pl.ds(2 * g * D, 2 * D)
+        store(o_ref.at[:, pair], o_hbm.at[0, :, pair], out_sem.at[0, g])
+        store(dq_ref.at[:, pair], dq_hbm.at[0, :, pair], out_sem.at[1, g])
+
+    part[0:1, :] = gq
+    part[1:2, :] = gk / k_gain
+
+    @pl.loop(1, nc * nd)
+    def _(d):
+        sum_copy(d).start()
 
     for g in range(KV):
         for off in range(1, HALO + 1):
@@ -204,9 +228,11 @@
                 grad_copy(g, off).wait_recv()
         col = pl.ds(g * D, D)
         acc = own[g] + grecv[0, g].astype(F32) + grecv[1, g].astype(F32)
-        k_hat, k_inv = hat(k_ref[0, :, col])
-        dk_ref[0, :, col] = norm_backward(acc[:, 0:D], k_hat, k_inv, k_gain).astype(BF16)
-        dv_ref[0, :, col] = acc[:, D:].astype(BF16)
+        k_hat, k_inv = hat(k_ref[:, col])
+        dk_ref[:, col] = norm_backward(acc[:, 0:D], k_hat, k_inv, k_gain).astype(BF16)
+        dv_ref[:, col] = acc[:, D:].astype(BF16)
+        store(dk_ref.at[:, col], dk_hbm.at[0, :, col], out_sem.at[2, g])
+        store(dv_ref.at[:, col], dv_hbm.at[0, :, col], out_sem.at[3, g])
 
     for off in range(1, HALO + 1):
         @pl.when(me + off < nc)
@@ -219,14 +245,40 @@
         def _(off=off):
             for g in range(KV):
                 grad_copy(g, off).wait_send()
-    pltpu.make_async_copy(stage_c, stage_c, r_send.at[0]).wait()
-    pltpu.make_async_copy(stage_d, stage_d, r_send.at[1]).wait()
+    pltpu.make_async_copy(stage, stage, r_send).wait()
+    pltpu.make_async_copy(stage, stage, r_recv).wait()
+    total = (part[...] + jnp.sum(stage[...], 0)) * float(nc * nd * T) ** (-0.5)
+    gq_ref[...] = total[0:1]
+    gk_ref[...] = total[1:2]
+    store(gq_ref, gq_hbm, gain_sem.at[0])
+    store(gk_ref, gk_hbm, gain_sem.at[1])
+    for copy in stores:
+        copy.wait()
+
+
+def deliver_kernel(*refs):
+    n = len(refs) // 2
+    sems = refs[-1]
+    copies = [pltpu.make_async_copy(refs[i], refs[n + i], sems.at[i]) for i in range(n)]
+    for copy in copies:
+        copy.start()
+    for copy in copies:
+        copy.wait()
+
+
+def deliver(*arrays):
+    return pl.pallas_call(
+        deliver_kernel,
+        out_shape=tuple(jax.ShapeDtypeStruct(a.shape, a.dtype) for a in arrays),
+        in_specs=[pl.BlockSpec(memory_space=pl.ANY)] * len(arrays),
+        out_specs=(pl.BlockSpec(memory_space=pl.ANY),) * len(arrays),
+        scratch_shapes=[pltpu.SemaphoreType.DMA((len(arrays),))],
+    )(*arrays)
 
 
 def body(nc, nd, queries, keys, values, q_gain, key_norm_gain, segment_ids, output_gradient):
     T = queries.shape[1]
     dma = pltpu.SemaphoreType.DMA
-    vmem = pl.BlockSpec(memory_space=pltpu.VMEM)
     outs = pl.pallas_call(
         functools.partial(kernel, nc, nd),
         out_shape=(
@@ -237,28 +289,40 @@
             jax.ShapeDtypeStruct((1, D), F32),
             jax.ShapeDtypeStruct((1, D), F32),
         ),
-        in_specs=[vmem] * 7,
-        out_specs=(vmem,) * 6,
+        in_specs=[pl.BlockSpec(memory_space=pl.ANY)] * 7,
+        out_specs=(pl.BlockSpec(memory_space=pl.ANY),) * 6,
         scratch_shapes=[
+            pltpu.VMEM((T, HEADS * D), BF16),
+            pltpu.VMEM((T, KV * D), BF16),
+            pltpu.VMEM((T, HEADS * D), BF16),
+            pltpu.VMEM((1, D), F32),
+            pltpu.VMEM((1, D), F32),
+            pltpu.VMEM((1, T), jnp.int32),
+            dma((2 * KV + 5,)),
+            pltpu.VMEM((T, HEADS * D), BF16),
+            pltpu.VMEM((T, HEADS * D), BF16),
+            pltpu.VMEM((T, KV * D), BF16),
+            pltpu.VMEM((T, KV * D), BF16),
+            pltpu.VMEM((1, D), F32),
+            pltpu.VMEM((1, D), F32),
+            dma((4, KV)), dma((2,)),
             pltpu.VMEM((KV, (HALO + 1) * T, 2 * D), BF16),
             pltpu.VMEM((HALO + 1, 8, T), jnp.int32),
             pltpu.VMEM((KV, HALO * T, 2 * D), BF16),
             pltpu.VMEM((HALO, KV, T, 2 * D), BF16),
             pltpu.VMEM((KV, T, 2 * D), F32),
             pltpu.VMEM((2, D), F32),
-            pltpu.VMEM((2, D), F32),
-            pltpu.VMEM((nc - 1, 2, D), F32),
-            pltpu.VMEM((nd - 1, 2, D), F32),
+            pltpu.VMEM((nc * nd - 1, 2, D), F32),
             dma((HALO, KV)), dma((HALO, KV)),
             dma((HALO,)), dma((HALO,)),
             dma((HALO, KV)), dma((HALO, KV)),
-            dma((2,)), dma((2,)),
+            dma, dma,
         ],
         compiler_params=pltpu.CompilerParams(
-            collective_id=0, has_side_effects=True, vmem_limit_bytes=48 * 1024 * 1024,
+            collective_id=0, has_side_effects=True, vmem_limit_bytes=63 * 1024 * 1024,
         ),
     )(queries, keys, values, q_gain.reshape(1, D), key_norm_gain.reshape(1, D), segment_ids, output_gradient)
-    attn_out, dq, dk, dv, gq, gk = outs
+    attn_out, dq, dk, dv, gq, gk = deliver(*outs)
     return attn_out, dq, dk, dv, gq.reshape(D), gk.reshape(D)
 
 

time: 49.3 us -> 89.4 us (1.81)
  Pallas kernels: 39.6 us -> 88.6 us
  local copies, waits for them, and re-layouts: 8.77 us -> 0 us
    pallas_call x0 -> x1, Pallas kernels: none -> 48.9 us  [deliver(): pl.pallas_call(deliver_kernel, out_shape=tuple((jax.ShapeDtypeStruct(a.sh...]
    unnamed x20 -> x0, local copies, waits for them, and re-layouts: 8.77 us -> none
where the time goes in v2:
time: 89.4 us; the launch traced here: 89.3 us
  Pallas kernels  88.6 us (99%)
    pallas_call x1, Pallas kernels, deliver(): pl.pallas_call(deliver_kernel, out_shape=tuple((jax.ShapeDtypeStruct(a.sh...  48.9 us
    pallas_call x1, Pallas kernels, body(): pl.pallas_call(functools.partial(kernel, nc, nd), out_shape=(jax.ShapeDty...  39.8 us

profile of v2, /device:TPU:0, one launch (start us, length us, event | category | flops | bytes accessed | tf_op | source)
XLA Modules:
  0.0 89.3 jit_solution(3168621128846105082)
XLA Ops:
  0.6 39.8 %shard_map.118 = (bf16[1,128,2048]{2,1,0:T(8,128)(2,1)}, bf16[1,128,2048]{2,1,0:T(8,128)(2,1)}, bf16[1,128,1024]{2,1,0:T(8,128)(2,1)}, bf16[1,128,1024]{2,1,0:T(...) custom-call(bf16[1,128,2048]{2,1,0:T(8,128)(2,1)} %q_hbm.1, bf16[1,128,1024]{2,1,0:T(8,128)(2,1)} %k_hbm.1, ...), custom_call_target="tpu_custom_call" | custom-call | tf_op jit(solution)/shard_map/pallas_call | solution.py:282
  40.4 48.9 %shard_map.119 = (bf16[1,128,2048]{2,1,0:T(8,128)(2,1)}, bf16[1,128,2048]{2,1,0:T(8,128)(2,1)}, bf16[1,128,1024]{2,1,0:T(8,128)(2,1)}, bf16[1,128,1024]{2,1,0:T(...) custom-call(bf16[1,128,2048]{2,1,0:T(8,128)(2,1)} %get-tuple-element.18.refs_0_, ...), custom_call_target="tpu_custom_call" | custom-call | tf_op jit(solution)/shard_map/pallas_call | solution.py:270

commit v3 on v2

--- a/solution.py
+++ b/solution.py
@@ -257,22 +257,31 @@
 
 
 def deliver_kernel(*refs):
-    n = len(refs) // 2
-    sems = refs[-1]
-    copies = [pltpu.make_async_copy(refs[i], refs[n + i], sems.at[i]) for i in range(n)]
-    for copy in copies:
+    n = (len(refs) - 2) // 3
+    ins, outs, held = refs[:n], refs[n:2 * n], refs[2 * n:3 * n]
+    in_sem, out_sem = refs[-2:]
+    loads = [pltpu.make_async_copy(ins[i], held[i], in_sem.at[i]) for i in range(n)]
+    stores = [pltpu.make_async_copy(held[i], outs[i], out_sem.at[i]) for i in range(n)]
+    for copy in loads:
         copy.start()
-    for copy in copies:
+    for i in range(n):
+        loads[i].wait()
+        stores[i].start()
+    for copy in stores:
         copy.wait()
 
 
 def deliver(*arrays):
+    n = len(arrays)
+    anywhere = pl.BlockSpec(memory_space=pl.ANY)
     return pl.pallas_call(
         deliver_kernel,
         out_shape=tuple(jax.ShapeDtypeStruct(a.shape, a.dtype) for a in arrays),
-        in_specs=[pl.BlockSpec(memory_space=pl.ANY)] * len(arrays),
-        out_specs=(pl.BlockSpec(memory_space=pl.ANY),) * len(arrays),
-        scratch_shapes=[pltpu.SemaphoreType.DMA((len(arrays),))],
+        in_specs=[anywhere] * n,
+        out_specs=(anywhere,) * n,
+        scratch_shapes=[pltpu.VMEM(a.shape, a.dtype) for a in arrays]
+        + [pltpu.SemaphoreType.DMA((n,))] * 2,
+        compiler_params=pltpu.CompilerParams(vmem_limit_bytes=63 * 1024 * 1024),
     )(*arrays)
 
 

time: 89.4 us -> 42.9 us (0.48)
  Pallas kernels: 88.6 us -> 42.1 us
    pallas_call x1, Pallas kernels: 48.9 us -> 2.29 us  [deliver(): pl.pallas_call(deliver_kernel, out_shape=tuple((jax.ShapeDtypeStruct(a.sh...]
where the time goes in v3:
time: 42.9 us; the launch traced here: 42.7 us
  Pallas kernels  42.1 us (98%)
  between operations  0.64 us (1%)
    pallas_call x1, Pallas kernels, body(): pl.pallas_call(functools.partial(kernel, nc, nd), out_shape=(jax.ShapeDty...  39.8 us
    pallas_call x1, Pallas kernels, deliver(): pl.pallas_call(deliver_kernel, out_shape=tuple((jax.ShapeDtypeStruct(a.sh...  2.29 us

profile of v3, /device:TPU:0, one launch (start us, length us, event | category | flops | bytes accessed | tf_op | source)
XLA Modules:
  0.0 42.7 jit_solution(8462356688977968563)
XLA Ops:
  0.6 39.8 %shard_map.118 = (bf16[1,128,2048]{2,1,0:T(8,128)(2,1)}, bf16[1,128,2048]{2,1,0:T(8,128)(2,1)}, bf16[1,128,1024]{2,1,0:T(8,128)(2,1)}, bf16[1,128,1024]{2,1,0:T(...) custom-call(bf16[1,128,2048]{2,1,0:T(8,128)(2,1)} %q_hbm.1, bf16[1,128,1024]{2,1,0:T(8,128)(2,1)} %k_hbm.1, ...), custom_call_target="tpu_custom_call" | custom-call | tf_op jit(solution)/shard_map/pallas_call | solution.py:291
  40.4 2.3 %shard_map.119 = (bf16[1,128,2048]{2,1,0:T(8,128)(2,1)}, bf16[1,128,2048]{2,1,0:T(8,128)(2,1)}, bf16[1,128,1024]{2,1,0:T(8,128)(2,1)}, bf16[1,128,1024]{2,1,0:T(...) custom-call(bf16[1,128,2048]{2,1,0:T(8,128)(2,1)} %get-tuple-element.18.refs_0_, ...), custom_call_target="tpu_custom_call" | custom-call | tf_op jit(solution)/shard_map/pallas_call | solution.py:277

commit v4 on v3

--- a/solution.py
+++ b/solution.py
@@ -40,12 +40,15 @@
     o_hbm, dq_hbm, dk_hbm, dv_hbm, gq_hbm, gk_hbm,
     q_ref, k_ref, do_ref, qg_ref, kg_ref, seg_ref, in_sem,
     o_ref, dq_ref, dk_ref, dv_ref, gq_ref, gk_ref, out_sem, gain_sem,
-    kvbuf, segbuf, gbuf, grecv, own, part, stage,
+    kvbuf, segbuf, gbuf, grecv, own, far, part, stage,
     kv_send, kv_recv, seg_send, seg_recv, g_send, g_recv, r_send, r_recv,
 ):
     T = k_hbm.shape[1]
     me = lax.axis_index("ctx")
     dpi = lax.axis_index("dp")
+    even = lax.rem(me, 2) == 0
+    odd = lax.rem(me, 2) == 1
+    middle = odd & (me > HALO)
 
     loads = {}
 
@@ -108,11 +111,27 @@
     def sum_copy(d):
         return remote(part, stage.at[d - 1], r_send, r_recv, peer_of(d))
 
-    def grad_copy(g, off):
+    def relay_copy(g):
         return remote(
-            gbuf.at[g, rows(HALO - off)], grecv.at[off - 1, g],
-            g_send.at[off - 1, g], g_recv.at[off - 1, g], {"ctx": me - off},
-        )
+            kvbuf.at[g, rows(0)], kvbuf.at[g, rows(1)], kv_send.at[0, g], kv_recv.at[0, g], {"ctx": me - 1},
+        )
+
+    def near_copy(g, to):
+        return remote(
+            gbuf.at[g, rows(1)], grecv.at[0, g], g_send.at[0, g], g_recv.at[0, g], {"ctx": me + to},
+        )
+
+    def far_copy(g):
+        return remote(
+            gbuf.at[g, rows(0)], grecv.at[1, g], g_send.at[1, g], g_recv.at[1, g], {"ctx": me - 2},
+        )
+
+    def pass_on(g):
+        @pl.when(middle)
+        def _():
+            near_copy(g, 1).wait_recv()
+            gbuf[g, rows(0)] = (far[g] + grecv[0, g].astype(F32)).astype(BF16)
+            far_copy(g).start()
 
     arrive("kg")
     k_gain = kg_ref[...]
@@ -130,10 +149,14 @@
                 @pl.when(me + off < nc)
                 def _(off=off):
                     seg_copy(off).start()
-        for off in range(1, HALO + 1):
-            @pl.when(me + off < nc)
-            def _(off=off, g=g):
-                kv_copy(g, off).start()
+
+        @pl.when(me + 2 < nc)
+        def _(g=g):
+            kv_copy(g, 2).start()
+
+        @pl.when(even)
+        def _(g=g):
+            kv_copy(g, 1).start()
 
     for off in range(1, HALO + 1):
         @pl.when(me < off)
@@ -142,10 +165,10 @@
                 kvbuf[g, rows(HALO - off)] = jnp.zeros((T, 2 * D), BF16)
             segbuf[HALO - off] = jnp.full((8, T), -1, jnp.int32)
 
-        @pl.when(me + off >= nc)
-        def _(off=off):
-            for g in range(KV):
-                grecv[off - 1, g] = jnp.zeros((T, 2 * D), BF16)
+    @pl.when(me + 2 >= nc)
+    def _():
+        for g in range(KV):
+            grecv[1, g] = jnp.zeros((T, 2 * D), BF16)
 
     arrive("qg")
     q_gain = qg_ref[...]
@@ -174,10 +197,17 @@
     gq = jnp.zeros((1, D), F32)
     gk = jnp.zeros((1, D), F32)
     for g in range(KV):
-        for off in range(1, HALO + 1):
-            @pl.when(me >= off)
-            def _(off=off, g=g):
-                kv_copy(g, off).wait_recv()
+        @pl.when(me >= 2)
+        def _(g=g):
+            kv_copy(g, 2).wait_recv()
+
+        @pl.when(middle)
+        def _(g=g):
+            relay_copy(g).start()
+
+        @pl.when(me >= 1)
+        def _(g=g):
+            kv_copy(g, 1).wait_recv()
         K = kvbuf[g, :, 0:D]
         V = kvbuf[g, :, D:]
         Q = jnp.concatenate([qs[2 * g], qs[2 * g + 1]], 0)
@@ -194,12 +224,22 @@
         ds = (prob * (dot(dO, V, (1, 1)) - delta)).astype(BF16)
         dK = dot(ds, Q, (0, 0))
         dV = dot(prob_b, dO, (0, 0))
-        gbuf[g, :, 0:D] = dK[:HALO * T].astype(BF16)
-        gbuf[g, :, D:] = dV[:HALO * T].astype(BF16)
-        for off in range(1, HALO + 1):
-            @pl.when(me >= off)
-            def _(off=off, g=g):
-                grad_copy(g, off).start()
+        gbuf[g, rows(1), 0:D] = dK[T:2 * T].astype(BF16)
+        gbuf[g, rows(1), D:] = dV[T:2 * T].astype(BF16)
+
+        @pl.when(even & (me >= 2))
+        def _(g=g, dK=dK, dV=dV):
+            near_copy(g, 1).start()
+            gbuf[g, rows(0), 0:D] = dK[:T].astype(BF16)
+            gbuf[g, rows(0), D:] = dV[:T].astype(BF16)
+            far_copy(g).start()
+
+        @pl.when(odd)
+        def _(g=g, dK=dK, dV=dV):
+            near_copy(g, -1).start()
+            far[g, :, 0:D] = dK[:T]
+            far[g, :, D:] = dV[:T]
+
         own[g, :, 0:D] = dK[HALO * T:]
         own[g, :, D:] = dV[HALO * T:]
         gk += jnp.sum(dK * K.astype(F32), 0, keepdims=True)
@@ -213,6 +253,8 @@
         pair = pl.ds(2 * g * D, 2 * D)
         store(o_ref.at[:, pair], o_hbm.at[0, :, pair], out_sem.at[0, g])
         store(dq_ref.at[:, pair], dq_hbm.at[0, :, pair], out_sem.at[1, g])
+        if g > 0:
+            pass_on(g - 1)
 
     part[0:1, :] = gq
     part[1:2, :] = gk / k_gain
@@ -221,13 +263,18 @@
     def _(d):
         sum_copy(d).start()
 
+    pass_on(KV - 1)
+
     for g in range(KV):
-        for off in range(1, HALO + 1):
-            @pl.when(me + off < nc)
-            def _(off=off, g=g):
-                grad_copy(g, off).wait_recv()
+        @pl.when(even)
+        def _(g=g):
+            near_copy(g, -1).wait_recv()
+
+        @pl.when(me + 2 < nc)
+        def _(g=g):
+            far_copy(g).wait_recv()
         col = pl.ds(g * D, D)
-        acc = own[g] + grecv[0, g].astype(F32) + grecv[1, g].astype(F32)
+        acc = own[g] + jnp.where(even, grecv[0, g].astype(F32), 0.0) + grecv[1, g].astype(F32)
         k_hat, k_inv = hat(k_ref[:, col])
         dk_ref[:, col] = norm_backward(acc[:, 0:D], k_hat, k_inv, k_gain).astype(BF16)
         dv_ref[:, col] = acc[:, D:].astype(BF16)
@@ -238,13 +285,27 @@
         @pl.when(me + off < nc)
         def _(off=off):
             seg_copy(off).wait_send()
-            for g in range(KV):
-                kv_copy(g, off).wait_send()
-
-        @pl.when(me >= off)
-        def _(off=off):
-            for g in range(KV):
-                grad_copy(g, off).wait_send()
+
+    @pl.when(me + 2 < nc)
+    def _():
+        for g in range(KV):
+            kv_copy(g, 2).wait_send()
+
+    @pl.when(even | middle)
+    def _():
+        for g in range(KV):
+            kv_copy(g, 1).wait_send()
+
+    @pl.when(me >= 2)
+    def _():
+        for g in range(KV):
+            far_copy(g).wait_send()
+
+    @pl.when(me >= 1)
+    def _():
+        for g in range(KV):
+            near_copy(g, 1).wait_send()
+
     pltpu.make_async_copy(stage, stage, r_send).wait()
     pltpu.make_async_copy(stage, stage, r_recv).wait()
     total = (part[...] + jnp.sum(stage[...], 0)) * float(nc * nd * T) ** (-0.5)
@@ -320,6 +381,7 @@
             pltpu.VMEM((KV, HALO * T, 2 * D), BF16),
             pltpu.VMEM((HALO, KV, T, 2 * D), BF16),
             pltpu.VMEM((KV, T, 2 * D), F32),
+            pltpu.VMEM((KV, T, 2 * D), F32),
             pltpu.VMEM((2, D), F32),
             pltpu.VMEM((nc * nd - 1, 2, D), F32),
             dma((HALO, KV)), dma((HALO, KV)),

time: 42.9 us -> 45.7 us (1.065)
  the two profiles are of different devices: /device:TPU:0 before, /device:TPU:2 now
where the time goes in v4:
time: 45.7 us; the launch traced here: 45.5 us
  Pallas kernels  44.9 us (98%)
  between operations  0.64 us (1%)
    pallas_call x1, Pallas kernels, body(): pl.pallas_call(functools.partial(kernel, nc, nd), out_shape=(jax.ShapeDty...  42.6 us
    pallas_call x1, Pallas kernels, deliver(): pl.pallas_call(deliver_kernel, out_shape=tuple((jax.ShapeDtypeStruct(a.sh...  2.29 us

profile of v4, /device:TPU:2, one launch (start us, length us, event | category | flops | bytes accessed | tf_op | source)
XLA Modules:
  0.0 45.5 jit_solution(12979477676760796506)
XLA Ops:
  0.6 42.6 %shard_map.118 = (bf16[1,128,2048]{2,1,0:T(8,128)(2,1)}, bf16[1,128,2048]{2,1,0:T(8,128)(2,1)}, bf16[1,128,1024]{2,1,0:T(8,128)(2,1)}, bf16[1,128,1024]{2,1,0:T(...) custom-call(bf16[1,128,2048]{2,1,0:T(8,128)(2,1)} %q_hbm.1, bf16[1,128,1024]{2,1,0:T(8,128)(2,1)} %k_hbm.1, ...), custom_call_target="tpu_custom_call" | custom-call | tf_op jit(solution)/shard_map/pallas_call | solution.py:352
  43.2 2.3 %shard_map.119 = (bf16[1,128,2048]{2,1,0:T(8,128)(2,1)}, bf16[1,128,2048]{2,1,0:T(8,128)(2,1)}, bf16[1,128,1024]{2,1,0:T(8,128)(2,1)}, bf16[1,128,1024]{2,1,0:T(...) custom-call(bf16[1,128,2048]{2,1,0:T(8,128)(2,1)} %get-tuple-element.18.refs_0_, ...), custom_call_target="tpu_custom_call" | custom-call | tf_op jit(solution)/shard_map/pallas_call | solution.py:338
